TPU v7x, 128 devices: a whole 4x4x4 slice. The times are simulated.
128 devices in a mesh: dp: 8 (over y, x_hi), tensor: 16 (over z, x_lo, core).
Axes of the slice: x: 4 (x_hi: 2, x_lo: 2; x = x_hi * 2 + x_lo), y: 4, z: 4, core: 2. Of those that a mesh axis runs over, the one named last changes fastest.
Arguments:
- prefill_rows: bfloat16 [8192, 8192], P(('dp', 'tensor')), parts along dimension 0, may hold values from -6 to 6
- decode_rows: bfloat16 [256, 8192], P(('dp', 'tensor')), parts along dimension 0, may hold values from -6 to 6
- norm_gain: bfloat16 [8192], replicated, may hold values from 0.099609375 to 1.8984375
- w_query: bfloat16 [8192, 8192], P(None, 'tensor'), may hold values from -0.0625 to 0.0625
- w_key: bfloat16 [8192, 1024], P(None, 'tensor'), may hold values from -0.0625 to 0.0625
- w_value: bfloat16 [8192, 1024], P(None, 'tensor'), may hold values from -0.0625 to 0.0625
- w_out: bfloat16 [8192, 8192], P('tensor'), may hold values from -0.0625 to 0.0625
- prefix_keys: bfloat16 [8192, 1024], P('dp', 'tensor'), parts along dimension 0
- prefix_values: bfloat16 [8192, 1024], P('dp', 'tensor'), parts along dimension 0, may hold values from -6 to 6
- prefill_start: int32 [8], P('dp'), parts along dimension 0, may hold values from 512 to 1024
- cache_keys: bfloat16 [256, 512, 1024], P(('dp', 'tensor')), parts along dimension 0
- cache_values: bfloat16 [256, 512, 1024], P(('dp', 'tensor')), parts along dimension 0, may hold values from -6 to 6
- cache_lengths: int32 [256], P(('dp', 'tensor')), parts along dimension 0, may hold values from 1 to 512, as said below
Outputs:
- prefill_out: bfloat16 [8192, 8192], P(('dp', 'tensor')), parts along dimension 0
- decode_out: bfloat16 [256, 8192], P(('dp', 'tensor')), parts along dimension 0
There are 8 independent parts, one for each index of `dp`. A program takes and returns all parts, laid end to end along the dimension named above; an argument that names none is the same for every part. Nothing has to cross between parts.
Inputs may be any that keep to these rules, and one draw needn't show every extreme that they name: `cache_lengths`: some decode row's cache holds exactly 512 positions.
All inputs are finite; a program needn't handle non-finite values.
Results may differ from a plain program's by a relative error of at most 0.024.
The roundings to bfloat16 on the way count: a program that leaves them out, or rounds other values in their place, can miss the bound.
Values may be sent and summed in bfloat16 or wider, within the bound.
No kernel may reach another device: no remote copies, remote signals or barrier semaphores. Data moves between devices by JAX's collectives and lax.ppermute only.
A program may use at most 192 MiB of HBM per device.

v0:
```python
import math

import jax
import jax.numpy as jnp
from jax import lax
from jax.sharding import PartitionSpec as P

HEAD_DIM = 128


def partner_2(block, axis, apart):
    count = lax.axis_size(axis)
    route = []
    for low in range(count):
        high = low | 1 << apart
        if high != low and high < count:
            route += [(low, high), (high, low)]
    return lax.ppermute(block, axis, route)


def rms_norm(rows, gain):
    widened = rows.astype(jnp.float32)
    mean_sq = jnp.mean(widened * widened, axis=-1, keepdims=True)
    return (widened * lax.rsqrt(mean_sq + 1e-05) * gain.astype(jnp.float32)).astype(jnp.bfloat16)


def rotate(values, positions):
    half_dim = values.shape[-1] // 2
    frequency = jnp.exp(
        jnp.arange(half_dim, dtype=jnp.float32) * (-2.0 * math.log(500000.0) / values.shape[-1])
    )
    angles = positions[..., None] * frequency
    cosine = jnp.cos(angles)
    sine_part = jnp.sin(angles)
    widened = values.astype(jnp.float32)
    first_half = widened[..., :half_dim]
    second_half = widened[..., half_dim:]
    return jnp.concatenate(
        [
            first_half * cosine - second_half * sine_part,
            second_half * cosine + first_half * sine_part,
        ],
        -1,
    ).astype(jnp.bfloat16)


def decode_attend(queries, new_keys, new_values, cached_keys, cached_values, lengths):
    rows = queries.shape[0]
    heads = queries.shape[1] // HEAD_DIM
    kv_heads = new_keys.shape[1] // HEAD_DIM
    group_size = heads // kv_heads
    score_scale = HEAD_DIM ** (-0.5)
    positions = lengths.astype(jnp.float32)
    q_rot = rotate(queries.reshape(rows, heads, HEAD_DIM), positions[:, None]).reshape(
        rows, kv_heads, group_size, HEAD_DIM
    )
    k_rot = rotate(new_keys.reshape(rows, kv_heads, HEAD_DIM), positions[:, None])
    v_new = new_values.reshape(rows, kv_heads, HEAD_DIM)
    span = cached_keys.shape[1]
    cache_k = cached_keys.reshape(rows, span, kv_heads, HEAD_DIM)
    cache_v = cached_values.reshape(rows, span, kv_heads, HEAD_DIM)
    old_scores = (
        jnp.einsum("rgjd,rlgd->rgjl", q_rot, cache_k, preferred_element_type=jnp.float32)
        * score_scale
    )
    valid = jnp.arange(span, dtype=jnp.int32)[None, :] < lengths[:, None]
    old_scores = jnp.where(valid[:, None, None, :], old_scores, -jnp.inf)
    own_score = (
        jnp.einsum("rgjd,rgd->rgj", q_rot, k_rot, preferred_element_type=jnp.float32) * score_scale
    )
    row_max = jnp.maximum(jnp.max(old_scores, axis=-1), own_score)
    old_weights = jnp.exp(old_scores - row_max[..., None])
    own_weight = jnp.exp(own_score - row_max)
    total_weight = jnp.sum(old_weights, axis=-1) + own_weight
    old_probs = (old_weights / total_weight[..., None]).astype(jnp.bfloat16)
    own_prob = (own_weight / total_weight).astype(jnp.bfloat16)
    mixed = jnp.einsum("rgjl,rlgd->rgjd", old_probs, cache_v, preferred_element_type=jnp.float32)
    mixed = (
        mixed + own_prob.astype(jnp.float32)[..., None] * v_new.astype(jnp.float32)[:, :, None, :]
    )
    return mixed.astype(jnp.bfloat16).reshape(rows, heads * HEAD_DIM)


def shards(
    prefill_rows,
    decode_rows,
    norm_gain,
    w_query,
    w_key,
    w_value,
    w_out,
    prefix_keys,
    prefix_values,
    prefill_start,
    cache_keys,
    cache_values,
    cache_lengths,
):
    devices = lax.axis_size("tensor")
    local_pre = prefill_rows.shape[0]
    local_dec = decode_rows.shape[0]
    per_device = local_pre + local_dec
    q_cols = w_query.shape[1]
    kv_cols = w_key.shape[1]
    local_heads = q_cols // HEAD_DIM
    score_scale = HEAD_DIM ** (-0.5)
    offset = prefill_start[0]
    joined = jnp.concatenate([prefill_rows, decode_rows], 0)
    normed = rms_norm(joined, norm_gain)
    project_normed = lax.all_gather(normed, "tensor", axis=0, tiled=True)
    projected = jnp.concatenate(
        [
            jnp.dot(project_normed, w_query, preferred_element_type=jnp.float32),
            jnp.dot(project_normed, w_key, preferred_element_type=jnp.float32),
            jnp.dot(project_normed, w_value, preferred_element_type=jnp.float32),
        ],
        1,
    ).astype(jnp.bfloat16)
    width_all = projected.shape[1]
    projected = projected.reshape(devices, per_device, width_all)
    pre_proj = projected[:, :local_pre].reshape(devices * local_pre, width_all)
    dec_proj = projected[:, local_pre:].reshape(devices * local_dec, width_all)
    q_pre_raw = pre_proj[:, :q_cols]
    k_pre_part = pre_proj[:, q_cols : q_cols + kv_cols]
    v_pre_part = pre_proj[:, q_cols + kv_cols :]
    partner = partner_2((k_pre_part, v_pre_part, prefix_keys, prefix_values), "tensor", 0)
    lower_half = lax.axis_index("tensor") % 2 == 0

    def whole_head(mine, theirs):
        return jnp.where(
            lower_half, jnp.concatenate([mine, theirs], 1), jnp.concatenate([theirs, mine], 1)
        )

    k_pre_full = whole_head(k_pre_part, partner[0])
    v_pre_full = whole_head(v_pre_part, partner[1])
    prefix_k_full = whole_head(prefix_keys, partner[2])
    prefix_v_full = whole_head(prefix_values, partner[3])
    total_pre = pre_proj.shape[0]
    prefix_len = prefix_keys.shape[0]
    pre_pos = (offset + jnp.arange(total_pre, dtype=jnp.int32)).astype(jnp.float32)
    q_pre = rotate(q_pre_raw.reshape(total_pre, local_heads, HEAD_DIM), pre_pos[:, None])
    k_pre = rotate(k_pre_full, pre_pos)
    all_keys = jnp.concatenate([prefix_k_full, k_pre], 0)
    all_values = jnp.concatenate([prefix_v_full, v_pre_full], 0)
    block_rows = min(512, total_pre)
    prefix_ok = jnp.arange(prefix_len, dtype=jnp.int32)[None, :] < offset

    def attend_block(block_index):
        first_row = block_index * block_rows
        query_block = lax.dynamic_slice_in_dim(q_pre, first_row, block_rows, 0)
        scores = (
            jnp.einsum("qhd,kd->hqk", query_block, all_keys, preferred_element_type=jnp.float32)
            * score_scale
        )
        row_index = first_row + jnp.arange(block_rows, dtype=jnp.int32)
        allowed = jnp.concatenate(
            [
                jnp.broadcast_to(prefix_ok, (block_rows, prefix_len)),
                jnp.arange(total_pre, dtype=jnp.int32)[None, :] <= row_index[:, None],
            ],
            1,
        )
        scores = jnp.where(allowed[None], scores, -jnp.inf)
        row_max = jnp.max(scores, axis=-1, keepdims=True)
        weights = jnp.exp(scores - row_max)
        probs = (weights / jnp.sum(weights, axis=-1, keepdims=True)).astype(jnp.bfloat16)
        return jnp.einsum(
            "hqk,kd->qhd", probs, all_values, preferred_element_type=jnp.float32
        ).astype(jnp.bfloat16)

    blocks = lax.map(attend_block, jnp.arange(total_pre // block_rows, dtype=jnp.int32))
    attn_pre = blocks.reshape(total_pre, q_cols)
    q_dec = dec_proj[:, :q_cols]
    k_dec = dec_proj[:, q_cols : q_cols + kv_cols]
    v_dec = dec_proj[:, q_cols + kv_cols :]
    q_rows, k_rows, v_rows = (
        lax.all_to_all(q_dec, "tensor", split_axis=0, concat_axis=1, tiled=True),
        lax.all_to_all(k_dec, "tensor", split_axis=0, concat_axis=1, tiled=True),
        lax.all_to_all(v_dec, "tensor", split_axis=0, concat_axis=1, tiled=True),
    )
    attn_rows = decode_attend(q_rows, k_rows, v_rows, cache_keys, cache_values, cache_lengths)
    attn_dec = lax.all_to_all(attn_rows, "tensor", split_axis=1, concat_axis=0, tiled=True)
    decode_out = lax.psum_scatter(
        jnp.dot(attn_dec, w_out, preferred_element_type=jnp.float32).astype(jnp.bfloat16),
        "tensor",
        scatter_dimension=0,
        tiled=True,
    )
    prefill_out = lax.psum_scatter(
        jnp.dot(attn_pre, w_out, preferred_element_type=jnp.float32).astype(jnp.bfloat16),
        "tensor",
        scatter_dimension=0,
        tiled=True,
    )
    return (prefill_out, decode_out)


def solution(mesh):
    in_specs = (
        P(("dp", "tensor"), None),
        P(("dp", "tensor"), None),
        P(),
        P(None, "tensor"),
        P(None, "tensor"),
        P(None, "tensor"),
        P("tensor", None),
        P("dp", "tensor"),
        P("dp", "tensor"),
        P("dp"),
        P(("dp", "tensor"), None, None),
        P(("dp", "tensor"), None, None),
        P(("dp", "tensor")),
    )
    out_specs = (P(("dp", "tensor"), None), P(("dp", "tensor"), None))
    return jax.shard_map(shards, mesh=mesh, in_specs=in_specs, out_specs=out_specs, check_vma=False)
```

profile of v0, /device:TPU:0, one launch (start us, length us, event | category | flops | bytes accessed | tf_op | source)
XLA Modules:
  0.0 556.8 jit_solution(11460012300230202607)
XLA Ops:
  7.2 0.9 convert_element_type.98
  8.1 1.6 fusion.33
  9.8 2.6 fusion.42
  14.4 1.0 maximum_select_fusion.2
  15.6 100.9 %all-gather.3.cloned.1.call-done = bf16[16,66,8192]{2,1,0:T(8,128)(2,1)} async-done(((bf16[1,66,8192]{2,1,0:T(8,128)(2,1)}), bf16[16,66,8192]{2,1,0:T(8,128)(2,1)}) %all-gather.3.cloned.1.call-update) | async-done | bytes 17301520 | tf_op jit(solution)/shard_map/all_gather | solution.py:110
  116.6 23.1 %reshape.253 = bf16[1056,8192]{1,0:T(8,128)(2,1)} reshape(bf16[16,66,8192]{2,1,0:T(8,128)(2,1)} %all-gather.3.cloned.1.call-done) | data formatting | bytes 34603008
  139.7 15.9 %convolution_convert_fusion.2 = bf16[1056,512]{1,0:T(8,128)(2,1)} fusion(bf16[1056,8192]{1,0:T(8,128)(2,1)} %reshape.253, bf16[8192,512]{1,0:T(8,128)(2,1)} %param.18), kind=kOutput, calls=%fused_computation.32 | convolution fusion | flops 8858910720 | bytes 26771456 | tf_op jit(solution)/shard_map/dot_general | solution.py:113
  155.7 1.5 concatenate.69
  157.2 12.2 %convolution_convert_fusion.4 = bf16[1056,64]{0,1:T(8,128)(2,1)} fusion(bf16[1056,8192]{1,0:T(8,128)(2,1)} %reshape.253, bf16[8192,64]{0,1:T(8,128)(2,1)} %param.19), kind=kOutput, calls=%fused_computation.39 | convolution fusion | flops 1107363840 | bytes 18485248 | tf_op jit(solution)/shard_map/dot_general | solution.py:114
  169.5 2.1 concatenate.70
  171.5 2.0 copy.62
  173.5 12.2 %convolution_convert_fusion.3 = bf16[1056,64]{0,1:T(8,128)(2,1)} fusion(bf16[1056,8192]{1,0:T(8,128)(2,1)} %reshape.253, bf16[8192,64]{0,1:T(8,128)(2,1)} %param.20), kind=kOutput, calls=%fused_computation.38 | convolution fusion | flops 1107363840 | bytes 18485248 | tf_op jit(solution)/shard_map/dot_general | solution.py:115
  185.7 2.1 concatenate.71
  187.8 2.0 copy.63
  189.8 1.5 pad_maximum_fusion.4
  191.2 2.4 pad_maximum_fusion
  193.7 0.8 reshape.245
  195.1 4.9 all-to-all-start.1
  200.1 1.4 slice.64
  201.5 1.6 slice_convert_fusion
  204.4 2.9 reshape.248
  207.3 5.7 %all-to-all-start.2 = ((bf16[16,2,64]{2,1,0:T(2,128)(2,1)}), bf16[16,2,64]{2,1,0:T(2,128)(2,1)S(1)}, u32[]{:S(2)}, u32[]{:S(2)}) async-start(bf16[16,2,64]{2,1,0:T(2,128)(2,1)} %bitcast.11), calls=%async_computation.3 | async-start | bytes 16384 | tf_op jit(solution)/shard_map/all_to_all | solution.py:179
  213.2 5.9 %all-to-all-done.2 = bf16[16,2,64]{2,1,0:T(2,128)(2,1)S(1)} async-done(((bf16[16,2,64]{2,1,0:T(2,128)(2,1)}), bf16[16,2,64]{2,1,0:T(2,128)(2,1)S(1)}, u32[]{:S(2)}, u32[]{:S(2)}) %all-to-all-start.2) | async-done | bytes 4128 | tf_op jit(solution)/shard_map/all_to_all | solution.py:179
  219.1 3.7 all-to-all-start
  223.0 5.6 %all-to-all-done = bf16[16,2,512]{2,1,0:T(2,128)(2,1)S(1)} async-done(((bf16[16,2,512]{2,1,0:T(2,128)(2,1)}), bf16[16,2,512]{2,1,0:T(2,128)(2,1)S(1)}, u32[]{:S(2)}, u32[]{:S(2)}) %all-to-all-start) | async-done | bytes 32800 | tf_op jit(solution)/shard_map/all_to_all | solution.py:177
  229.0 0.8 fusion.81
  231.5 3.5 all-to-all-start.3
  235.0 3.2 fusion.78
  238.2 2.8 all-to-all-done.3
  241.0 5.8 %convolution_convert_fusion.1 = bf16[32,8192]{1,0:T(8,128)(2,1)} fusion(bf16[32,512]{1,0:T(8,128)(2,1)S(1)} %all_to_all.53, bf16[512,8192]{1,0:T(8,128)(2,1)} %param.21), kind=kOutput, calls=%fused_computation.31 | convolution fusion | flops 268697600 | bytes 8945664 | tf_op jit(solution)/shard_map/dot_general | solution.py:184
  246.9 1.3 maximum_select_fusion.3
  248.2 0.8 pad_maximum_fusion.3
  249.1 1.9 fusion.57
  251.0 2.3 subtract_convert_fusion.1
  254.5 1.0 maximum_maximum_fusion
  255.5 46.2 %while.11 = (s32[]{:T(128)}, bf16[2,512,4,128]{3,2,1,0:T(4,128)(2,1)}, s32[2]{0:T(128)S(1)}, bf16[1024,4,128]{2,0,1:T(8,128)(2,1)S(1)}, bf16[2048,128]{1,0:T(8,1...) while((s32[]{:T(128)}, ...), condition=%wide.region_4.5_spmd.clone, body=%wide.region_1.4_spmd.clone.sunk | while | flops 2174488064 | bytes 48261368 | solution.py:171
  257.1 0.7 compare_reduce_fusion.2
  258.4 10.5 %fusion.101 = (f32[4,512]{1,0:T(4,128)S(1)}, f32[4,512,2048]{2,1,0:T(8,128)}) fusion(pred[512,2048]{1,0:T(8,128)(4,1)S(1)} %pad_add_fusion.2, bf16[2048,128]{1,0:T(8,128)(2,1)} %get-tuple-element.170, bf16[1024,4,128]{2,0,1:T(8,128)(2,1)S(1)} %get-tuple-element.169, s32[]{:T(128)S(6)} %select_n.77), kind=kOutput, calls=%fused_computation.103.clone.1 | convolution fusion | flops 1090521088 | bytes 18882564 | tf_op jit(solution)/shard_map/while/body/eval_jaxpr/sub | solution.py:165
  268.8 8.3 %fusion.102 = bf16[1,512,4,128]{3,1,2,0:T(8,128)(2,1)S(1)} fusion(f32[4,512,2048]{2,1,0:T(8,128)} %get-tuple-element.140, f32[4,512]{1,0:T(4,128)S(1)} %get-tuple-element.141, bf16[2048,128]{1,0:T(8,128)(2,1)S(1)} %get-tuple-element.171), kind=kOutput, calls=%fused_computation.16.clone.1 | convolution fusion | flops 1082392576 | bytes 17833984 | tf_op jit(solution)/shard_map/while/body/eval_jaxpr/hqk,kd->qhd/dot_general | solution.py:167
  277.6 1.0 copy-done.14
  280.2 0.7 compare_reduce_fusion.2
  281.4 10.4 %fusion.101 = (f32[4,512]{1,0:T(4,128)S(1)}, f32[4,512,2048]{2,1,0:T(8,128)}) fusion(pred[512,2048]{1,0:T(8,128)(4,1)S(1)} %pad_add_fusion.2, bf16[2048,128]{1,0:T(8,128)(2,1)} %get-tuple-element.170, bf16[1024,4,128]{2,0,1:T(8,128)(2,1)S(1)} %get-tuple-element.169, s32[]{:T(128)S(6)} %select_n.77), kind=kOutput, calls=%fused_computation.103.clone.1 | convolution fusion | flops 1090521088 | bytes 18882564 | tf_op jit(solution)/shard_map/while/body/eval_jaxpr/sub | solution.py:165
  291.9 8.3 %fusion.102 = bf16[1,512,4,128]{3,1,2,0:T(8,128)(2,1)S(1)} fusion(f32[4,512,2048]{2,1,0:T(8,128)} %get-tuple-element.140, f32[4,512]{1,0:T(4,128)S(1)} %get-tuple-element.141, bf16[2048,128]{1,0:T(8,128)(2,1)S(1)} %get-tuple-element.171), kind=kOutput, calls=%fused_computation.16.clone.1 | convolution fusion | flops 1082392576 | bytes 17833984 | tf_op jit(solution)/shard_map/while/body/eval_jaxpr/hqk,kd->qhd/dot_general | solution.py:167
  300.7 1.0 copy-done.14
  301.7 14.8 %convolution_convert_fusion = bf16[1024,8192]{1,0:T(8,128)(2,1)} fusion(bf16[512,8192]{1,0:T(8,128)(2,1)} %param.21, bf16[128,8,4,128]{3,2,1,0:T(4,128)(2,1)} %bitcast.114), kind=kOutput, calls=%fused_computation.30 | convolution fusion | flops 8598323200 | bytes 26214400 | tf_op jit(solution)/shard_map/dot_general | solution.py:190
  318.4 45.6 %all-reduce.3.cloned.1.call-done = bf16[32,8192]{1,0:T(8,128)(2,1)} async-done(((bf16[32,8192]{1,0:T(8,128)(2,1)}), bf16[32,8192]{1,0:T(8,128)(2,1)}) %all-reduce.3.cloned.1.call-update) | async-done | bytes 524304
  364.0 1.6 constant_dynamic-slice_fusion
  365.5 184.7 %reduce-scatter.2.cloned.1.call-done = bf16[64,8192]{1,0:T(8,128)(2,1)} async-done(((bf16[1024,8192]{1,0:T(8,128)(2,1)}), bf16[64,8192]{1,0:T(8,128)(2,1)}) %reduce-scatter.2.cloned.1.call-update) | async-done | bytes 1048592 | tf_op jit(solution)/shard_map/reduce_scatter | solution.py:189
  (99 shorter events, 12.3 us)
Async XLA Ops:
  7.2 221.8 %copy-start = (bf16[2,512,1024]{2,1,0:T(8,128)(2,1)S(1)}, bf16[2,512,1024]{2,1,0:T(8,128)(2,1)}, u32[]{:S(2)}) copy-start(bf16[2,512,1024]{2,1,0:T(8,128)(2,1)} %param.25) | copy-start | bytes 6291460
  7.2 5.2 copy-start.7
  7.2 109.4 %all-gather.3.cloned.1.call-start = ((), (), s32[]{:S(2)}) async-start(), calls=%async_computation.6 | async-start | bytes 20054016 | tf_op jit(solution)/shard_map/all_gather | solution.py:110
  8.1 4.6 copy-start.8
  9.7 3.7 copy-start.11
  12.6 1.8 collective-permute-start.2
  12.9 2.5 collective-permute-start
  13.5 126.3 %copy-start.9 = (f32[64]{0:T(128)}, f32[64]{0:T(128)S(1)}, u32[]{:S(2)}) copy-start(f32[64]{0:T(128)S(1)} %multiply_exponential_fusion) | copy-start | bytes 772
  195.1 12.2 %all-to-all-start.1 = ((bf16[16,2,64]{2,1,0:T(2,128)(2,1)}), bf16[16,2,64]{2,1,0:T(2,128)(2,1)S(1)}, u32[]{:S(2)}, u32[]{:S(2)}) async-start(bf16[16,2,64]{2,1,0:T(2,128)(2,1)} %bitcast.6), calls=%async_computation.2 | async-start | bytes 16384 | tf_op jit(solution)/shard_map/all_to_all | solution.py:178
  203.9 43.0 %collective-permute-start.3 = (bf16[1024,64]{1,0:T(8,128)(2,1)S(1)}, bf16[1024,64]{1,0:T(8,128)(2,1)}, u32[]{:S(2)}, u32[]{:S(2)}) collective-permute-start(bf16[1024,64]{1,0:T(8,128)(2,1)S(1)} %get-tuple-element.77), channel_id=1, source_target_pairs={{0,1},{1,0},{2,3},{3,2},{4,5},{5,4},{6,7},{7,6},{8,9},{9,8},{10,11... | collective-permute-start | bytes 393224 | tf_op jit(solution)/shard_map/ppermute | solution.py:18
  204.3 44.8 %collective-permute-start.1 = (bf16[1024,64]{1,0:T(8,128)(2,1)S(1)}, bf16[1024,64]{1,0:T(8,128)(2,1)}, u32[]{:S(2)}, u32[]{:S(2)}) collective-permute-start(bf16[1024,64]{1,0:T(8,128)(2,1)S(1)} %get-tuple-element.78), channel_id=1, source_target_pairs={{0,1},{1,0},{2,3},{3,2},{4,5},{5,4},{6,7},{7,6},{8,9},{9,8},{10,11... | collective-permute-start | bytes 393224 | tf_op jit(solution)/shard_map/ppermute | solution.py:18
  207.3 11.8 %all-to-all-start.2 = ((bf16[16,2,64]{2,1,0:T(2,128)(2,1)}), bf16[16,2,64]{2,1,0:T(2,128)(2,1)S(1)}, u32[]{:S(2)}, u32[]{:S(2)}) async-start(bf16[16,2,64]{2,1,0:T(2,128)(2,1)} %bitcast.11), calls=%async_computation.3 | async-start | bytes 16384 | tf_op jit(solution)/shard_map/all_to_all | solution.py:179
  219.1 9.5 %all-to-all-start = ((bf16[16,2,512]{2,1,0:T(2,128)(2,1)}), bf16[16,2,512]{2,1,0:T(2,128)(2,1)S(1)}, u32[]{:S(2)}, u32[]{:S(2)}) async-start(bf16[16,2,512]{2,1,0:T(2,128)(2,1)} %all_to_all.44), calls=%async_computation.1 | async-start | bytes 65536 | tf_op jit(solution)/shard_map/all_to_all | solution.py:177
  228.7 1.6 copy-start.12
  229.8 5.3 copy-start.2
  231.5 9.5 %all-to-all-start.3 = ((bf16[2,16,512]{2,0,1:T(2,128)(2,1)}), bf16[2,16,512]{2,0,1:T(2,128)(2,1)S(1)}, u32[]{:S(2)}, u32[]{:S(2)}) async-start(bf16[2,16,512]{2,0,1:T(2,128)(2,1)} %copy.78), calls=%async_computation.4 | async-start | bytes 65536 | tf_op jit(solution)/shard_map/all_to_all | solution.py:182
  235.0 129.0 %all-reduce.3.cloned.1.call-start = ((), (), s32[]{:S(2)}) async-start(), calls=%async_computation.7 | async-start | bytes 1048576
  241.0 7.2 %copy-start.5 = (bf16[1024,128]{1,0:T(8,128)(2,1)S(1)}, bf16[1024,128]{1,0:T(8,128)(2,1)}, u32[]{:S(2)}) copy-start(bf16[1024,128]{1,0:T(8,128)(2,1)} %maximum_select_fusion.2) | copy-start | bytes 786436
  246.8 4.2 copy-start.10
  246.8 303.4 %reduce-scatter.2.cloned.1.call-start = ((), (), s32[]{:S(2)}) async-start(), calls=%async_computation.5 | async-start | bytes 17825792 | tf_op jit(solution)/shard_map/reduce_scatter | solution.py:189
  248.2 5.1 copy-start.3
  248.2 5.1 copy-start.4
  253.9 1.6 copy-start.6
  268.8 8.3 %copy-start.13 = (bf16[2,512,4,128]{3,2,1,0:T(4,128)(2,1)S(1)}, bf16[2,512,4,128]{3,2,1,0:T(4,128)(2,1)}, u32[]{:S(2)}) copy-start(bf16[2,512,4,128]{3,2,1,0:T(4,128)(2,1)} %get-tuple-element.155) | copy-start | bytes 3145732 | tf_op jit(solution)/shard_map/while
  277.6 1.0 copy-start.14
  291.9 8.3 %copy-start.13 = (bf16[2,512,4,128]{3,2,1,0:T(4,128)(2,1)S(1)}, bf16[2,512,4,128]{3,2,1,0:T(4,128)(2,1)}, u32[]{:S(2)}) copy-start(bf16[2,512,4,128]{3,2,1,0:T(4,128)(2,1)} %get-tuple-element.155) | copy-start | bytes 3145732 | tf_op jit(solution)/shard_map/while
  300.7 1.0 copy-start.14
  316.5 0.7 copy-start.15
  316.5 233.8 %copy-start.1 = (bf16[2,512,1024]{2,1,0:T(8,128)(2,1)S(1)}, bf16[2,512,1024]{2,1,0:T(8,128)(2,1)}, u32[]{:S(2)}) copy-start(bf16[2,512,1024]{2,1,0:T(8,128)(2,1)} %param.25) | copy-start | bytes 6291460
Sparse Core Ops, SparseCore 0:
  12.5 103.9 all-gather.2
  247.0 116.9 all-reduce.2
  367.1 183.1 reduce-scatter.1
where the time goes:
time: 558 us; the launch traced here: 557 us
  waiting for transfers between devices  346 us (62%)
  matrix products  100 us (18%)
  local copies, waits for them, and re-layouts  50.8 us (9%)
  other arithmetic  24.3 us (4%)
  starting transfers between devices  19.2 us (3%)
  between operations  15.5 us (3%)
    reduce_scatter x1, waiting for transfers between devices, shards(): lax.psum_scatter(jnp.dot(attn_pre, w_out, preferred_element_type=jnp.floa...  185 us
    all_gather x1, waiting for transfers between devices, shards(): project_normed = lax.all_gather(normed, 'tensor', axis=0, tiled=True)  101 us
    unnamed x4, waiting for transfers between devices  45.7 us
    unnamed x33, local copies, waits for them, and re-layouts  26.6 us
    sub x2, matrix products, attend_block(): weights = jnp.exp(scores - row_max)  20.9 us
    dot_general x2, matrix products, attend_block(): jnp.einsum('hqk,kd->qhd', probs, all_values, preferred_element_type=jnp.f...  16.6 us
    dot_general x1, matrix products, shards(): jnp.dot(project_normed, w_query, preferred_element_type=jnp.float32)  15.9 us
    dot_general x1, matrix products, shards(): jnp.dot(attn_pre, w_out, preferred_element_type=jnp.float32)  14.8 us
  transfers between devices with their start and end apart: 11, of which 6 were waited for; matrix products, arithmetic and copies ran while one was open for 16% of the time, Pallas kernels for 0%

commit v1 on v0

v1 whole, which is shorter than its diff:
```python
import functools
import math

import jax
import jax.numpy as jnp
from jax import lax
from jax.experimental import pallas as pl
from jax.experimental.pallas import tpu as pltpu
from jax.sharding import PartitionSpec as P

HEAD_DIM = 128
RING = 4
BF16 = jnp.bfloat16
F32 = jnp.float32
NT = (((1,), (1,)), ((), ()))


def route(move):
    pairs = []
    for z in range(RING):
        for x in range(2):
            for c in range(2):
                z2, x2, c2 = move(z, x, c)
                pairs.append(((z * 2 + x) * 2 + c, ((z2 % RING) * 2 + x2) * 2 + c2))
    return pairs


UP = route(lambda z, x, c: (z + 1, x, c))
DOWN = route(lambda z, x, c: (z - 1, x, c))
SIDE = route(lambda z, x, c: (z, 1 - x, c))
CORE = route(lambda z, x, c: (z, x, 1 - c))
SAME_CORE = [list(range(0, 4 * RING, 2)), list(range(1, 4 * RING, 2))]


def up(block):
    return lax.ppermute(block, "tensor", UP)


def down(block):
    return lax.ppermute(block, "tensor", DOWN)


def side(block):
    return lax.ppermute(block, "tensor", SIDE)


def swap(block):
    return lax.ppermute(block, "tensor", CORE)


def exchange(block):
    return lax.all_to_all(
        block, "tensor", split_axis=0, concat_axis=0, axis_index_groups=SAME_CORE, tiled=True
    )


def rms_norm(rows, gain):
    widened = rows.astype(F32)
    mean_sq = jnp.mean(widened * widened, axis=-1, keepdims=True)
    return (widened * lax.rsqrt(mean_sq + 1e-05) * gain.astype(F32)).astype(BF16)


def norm_kernel(a_ref, b_ref, gain_ref, a_out, b_out):
    gain = gain_ref[...]
    a_out[...] = rms_norm(a_ref[...], gain)
    b_out[...] = rms_norm(b_ref[...], gain)


def norm_halves(rows, gain):
    count, width = rows.shape
    half = count // 2
    step = 16
    steps = half // step
    return pl.pallas_call(
        norm_kernel,
        grid=(steps,),
        in_specs=[
            pl.BlockSpec((step, width), lambda i: (i, 0)),
            pl.BlockSpec((step, width), lambda i: (i + steps, 0)),
            pl.BlockSpec((1, width), lambda i: (0, 0)),
        ],
        out_specs=[pl.BlockSpec((step, width), lambda i: (i, 0))] * 2,
        out_shape=[jax.ShapeDtypeStruct((half, width), BF16)] * 2,
        name="norm_halves",
    )(rows, rows, gain.reshape(1, width))


def turn(values, cosine, signed_sine):
    widened = values.astype(F32)
    return (widened * cosine + pltpu.roll(widened, 64, 1) * signed_sine).astype(BF16)


def project_kernel(pieces, turned, core_ref, *refs):
    xs = refs[:pieces]
    wq_own, wq_other, wkv_own, wkv_other, cos_ref, sin_ref, q_out, kv_out, acc = refs[pieces:]
    step = pl.program_id(0)
    x = jnp.concatenate([r[...] for r in xs], axis=0) if pieces > 1 else xs[0][...]
    own_low = core_ref[0] == 0
    own, other = wkv_own[...], wkv_other[...]
    low = jnp.where(own_low, own, other)
    high = jnp.where(own_low, other, own)
    wkv = jnp.concatenate([low[:64], high[:64], low[64:], high[64:]], axis=0)
    cols = wq_own.shape[1]

    @pl.when(step == 0)
    def _():
        acc[...] = jnp.zeros_like(acc)

    acc[:, :cols] += jnp.dot(x, wq_own[...], preferred_element_type=F32)
    acc[:, cols : 2 * cols] += jnp.dot(x, wq_other[...], preferred_element_type=F32)
    acc[:, 2 * cols :] += lax.dot_general(x, wkv, NT, preferred_element_type=F32)

    @pl.when(step == pl.num_programs(0) - 1)
    def _():
        cosine, sine = cos_ref[...], sin_ref[...]
        total = acc.shape[0]
        for head in range(2 * cols // HEAD_DIM):
            at = slice(head * HEAD_DIM, (head + 1) * HEAD_DIM)
            raw = acc[:, at].astype(BF16)
            q_out[:turned, at] = turn(raw[:turned], cosine, sine)
            if total > turned:
                q_out[turned:, at] = raw[turned:]
        raw = acc[:, 2 * cols :].astype(BF16)
        kv_out[:turned, :HEAD_DIM] = turn(raw[:turned, :HEAD_DIM], cosine, sine)
        kv_out[:turned, HEAD_DIM:] = raw[:turned, HEAD_DIM:]
        if total > turned:
            kv_out[turned:, :] = raw[turned:]


def project(xs, turned, core, wq_own, wq_other, wkv_own, wkv_other, cosine, sine, name):
    total = sum(x.shape[0] for x in xs)
    width = xs[0].shape[1]
    cols = wq_own.shape[1]
    deep = 1024
    flops = 2 * total * width * (2 * cols + 256)
    return pl.pallas_call(
        functools.partial(project_kernel, len(xs), turned),
        grid_spec=pltpu.PrefetchScalarGridSpec(
            num_scalar_prefetch=1,
            grid=(width // deep,),
            in_specs=[pl.BlockSpec((x.shape[0], deep), lambda k, s: (0, k)) for x in xs]
            + [
                pl.BlockSpec((deep, cols), lambda k, s: (k, 0)),
                pl.BlockSpec((deep, cols), lambda k, s: (k, 0)),
                pl.BlockSpec((128, deep), lambda k, s: (0, k)),
                pl.BlockSpec((128, deep), lambda k, s: (0, k)),
                pl.BlockSpec((turned, HEAD_DIM), lambda k, s: (0, 0)),
                pl.BlockSpec((turned, HEAD_DIM), lambda k, s: (0, 0)),
            ],
            out_specs=[
                pl.BlockSpec((total, 2 * cols), lambda k, s: (0, 0)),
                pl.BlockSpec((total, 256), lambda k, s: (0, 0)),
            ],
            scratch_shapes=[pltpu.VMEM((total, 2 * cols + 256), F32)],
        ),
        out_shape=[
            jax.ShapeDtypeStruct((total, 2 * cols), BF16),
            jax.ShapeDtypeStruct((total, 256), BF16),
        ],
        compiler_params=pltpu.CompilerParams(vmem_limit_bytes=32 << 20),
        cost_estimate=pl.CostEstimate(
            flops=flops, bytes_accessed=2 * (total * width + width * (2 * cols + 256)), transcendentals=0
        ),
        name=name,
    )(core, *xs, wq_own, wq_other, wkv_own, wkv_other, cosine, sine)


def attend_kernel(blocks, prefix, spec_ref, q_ref, pk_ref, pv_ref, *refs):
    own_refs, other_refs = refs[:2], refs[2:4]
    out_ref, k_all, v_all = refs[4:]
    first = jnp.logical_and(pl.program_id(0) == 0, pl.program_id(1) == 0)
    rows = out_ref.shape[0]

    @pl.when(first)
    def _():
        k_all[:prefix] = pk_ref[...]
        v_all[:prefix, :HEAD_DIM] = pv_ref[...]
        v_all[:, HEAD_DIM:] = jnp.ones((v_all.shape[0], HEAD_DIM), BF16)
        for j in range(2 * RING):
            place = spec_ref[1 + j]
            for refs_here, at in ((own_refs, place), (other_refs, place ^ 1)):
                block = refs_here[j // RING][(j % RING) * rows : (j % RING + 1) * rows, :]
                here = pl.ds(pl.multiple_of(prefix + at * rows, rows), rows)
                k_all[here, :] = block[:, :HEAD_DIM]
                v_all[here, :HEAD_DIM] = block[:, HEAD_DIM:]

    place = spec_ref[1 + 2 * RING + pl.program_id(0)]
    start = spec_ref[0]
    heads = q_ref.shape[1] // HEAD_DIM
    group = 4 * rows
    for level in range(RING):

        @pl.when(place // 4 == level)
        def _():
            keys = prefix + group * (level + 1)
            q = jnp.concatenate(
                [q_ref[:, h * HEAD_DIM : (h + 1) * HEAD_DIM] for h in range(heads)], axis=0
            )
            scores = lax.dot_general(q, k_all[:keys, :], NT, preferred_element_type=F32) * (
                HEAD_DIM**-0.5
            )
            half = prefix // 2
            last = keys - group
            col = lax.broadcasted_iota(jnp.int32, (heads * rows, half), 1) + half
            late = jnp.where(col < start, scores[:, half:prefix], -jnp.inf)
            row = lax.broadcasted_iota(jnp.int32, (heads * rows, group), 0) % rows
            own_col = lax.broadcasted_iota(jnp.int32, (heads * rows, group), 1)
            diag = jnp.where(
                own_col <= row + (place % 4) * rows, scores[:, last:], -jnp.inf
            )
            parts = [scores[:, :half], late]
            if last > prefix:
                parts.append(scores[:, prefix:last])
            parts.append(diag)
            top = functools.reduce(
                jnp.maximum, [jnp.max(p, axis=1, keepdims=True) for p in parts]
            )
            probs = jnp.concatenate([jnp.exp(p - top).astype(BF16) for p in parts], axis=1)
            mixed = jnp.dot(probs, v_all[:keys, :], preferred_element_type=F32)
            out = (mixed[:, :HEAD_DIM] / mixed[:, HEAD_DIM:]).astype(BF16)
            for h in range(heads):
                out_ref[:, h * HEAD_DIM : (h + 1) * HEAD_DIM] = out[h * rows : (h + 1) * rows]


def attend(spec, q, prefix_k, prefix_v, own, other, rows, name):
    prefix = prefix_k.shape[0]
    width = q.shape[1]
    blocks = RING
    total = prefix + 4 * RING * rows

    def whole(a):
        return pl.BlockSpec(a.shape, lambda i, g, s: (0, 0))

    return pl.pallas_call(
        functools.partial(attend_kernel, blocks, prefix),
        grid_spec=pltpu.PrefetchScalarGridSpec(
            num_scalar_prefetch=1,
            grid=(blocks, 2),
            in_specs=[
                pl.BlockSpec((rows, width // 2), lambda i, g, s: (i, g)),
                whole(prefix_k),
                whole(prefix_v),
            ]
            + [whole(a) for a in own + other],
            out_specs=pl.BlockSpec((rows, width // 2), lambda i, g, s: (i, g)),
            scratch_shapes=[
                pltpu.VMEM((total, HEAD_DIM), BF16),
                pltpu.VMEM((total, 2 * HEAD_DIM), BF16),
            ],
        ),
        out_shape=jax.ShapeDtypeStruct((blocks * rows, width), BF16),
        compiler_params=pltpu.CompilerParams(vmem_limit_bytes=48 << 20),
        cost_estimate=pl.CostEstimate(
            flops=4 * blocks * rows * width * total,
            bytes_accessed=2 * (2 * blocks * rows * width + 3 * total * HEAD_DIM),
            transcendentals=blocks * rows * width // HEAD_DIM * total,
        ),
        name=name,
    )(spec, q, prefix_k, prefix_v, *own, *other)


def emit_kernel(inputs, sizes, *refs):
    xs, (own_ref, other_ref), outs = refs[:inputs], refs[inputs : inputs + 2], refs[inputs + 2 :]
    half = own_ref.shape[0]
    x = jnp.concatenate([r[...] for r in xs], axis=0) if inputs > 1 else xs[0][...]
    partial = jnp.dot(x[:, :half], own_ref[...], preferred_element_type=F32) + jnp.dot(
        x[:, half:], other_ref[...], preferred_element_type=F32
    )
    partial = partial.astype(BF16)
    at = 0
    for out, size in zip(outs, sizes):
        out[...] = partial[at : at + size]
        at += size


def emit(xs, own, other, sizes, name):
    total = sum(x.shape[0] for x in xs)
    half, width = own.shape
    wide = 1024
    return pl.pallas_call(
        functools.partial(emit_kernel, len(xs), tuple(sizes)),
        grid=(width // wide,),
        in_specs=[pl.BlockSpec(x.shape, lambda n: (0, 0)) for x in xs]
        + [pl.BlockSpec((half, wide), lambda n: (0, n))] * 2,
        out_specs=[pl.BlockSpec((size, wide), lambda n: (0, n)) for size in sizes],
        out_shape=[jax.ShapeDtypeStruct((size, width), BF16) for size in sizes],
        compiler_params=pltpu.CompilerParams(vmem_limit_bytes=32 << 20),
        cost_estimate=pl.CostEstimate(
            flops=4 * total * half * width,
            bytes_accessed=2 * (total * (2 * half + width) + 2 * half * width),
            transcendentals=0,
        ),
        name=name,
    )(*xs, own, other)


def frequencies():
    half_dim = HEAD_DIM // 2
    return jnp.exp(
        jnp.arange(half_dim, dtype=F32) * (-2.0 * math.log(500000.0) / HEAD_DIM)
    )


def tables(positions):
    angles = positions.astype(F32)[:, None] * frequencies()
    cosine, sine = jnp.cos(angles), jnp.sin(angles)
    return jnp.concatenate([cosine, cosine], 1), jnp.concatenate([-sine, sine], 1)


def rotate(values, positions):
    half_dim = values.shape[-1] // 2
    angles = positions[..., None] * frequencies()
    cosine, sine = jnp.cos(angles), jnp.sin(angles)
    widened = values.astype(F32)
    first, second = widened[..., :half_dim], widened[..., half_dim:]
    return jnp.concatenate(
        [first * cosine - second * sine, second * cosine + first * sine], -1
    ).astype(BF16)


def decode_attend(queries, new_keys, new_values, cached_keys, cached_values, lengths):
    rows, kv_heads, group_size, _ = queries.shape
    scale = HEAD_DIM**-0.5
    positions = lengths.astype(F32)
    q_rot = rotate(queries, positions[:, None, None])
    k_rot = rotate(new_keys, positions[:, None])
    span = cached_keys.shape[1]
    cache_k = cached_keys.reshape(rows, span, kv_heads, HEAD_DIM)
    cache_v = cached_values.reshape(rows, span, kv_heads, HEAD_DIM)
    old = jnp.einsum("rgjd,rlgd->rgjl", q_rot, cache_k, preferred_element_type=F32) * scale
    valid = jnp.arange(span, dtype=jnp.int32)[None, :] < lengths[:, None]
    old = jnp.where(valid[:, None, None, :], old, -jnp.inf)
    own = jnp.einsum("rgjd,rgd->rgj", q_rot, k_rot, preferred_element_type=F32) * scale
    top = jnp.maximum(jnp.max(old, axis=-1), own)
    old_weights = jnp.exp(old - top[..., None])
    own_weight = jnp.exp(own - top)
    total = jnp.sum(old_weights, axis=-1) + own_weight
    old_probs = (old_weights / total[..., None]).astype(BF16)
    own_prob = (own_weight / total).astype(BF16)
    mixed = jnp.einsum("rgjl,rlgd->rgjd", old_probs, cache_v, preferred_element_type=F32)
    mixed = mixed + own_prob.astype(F32)[..., None] * new_values.astype(F32)[:, :, None, :]
    return mixed.astype(BF16)


def add(*terms):
    return functools.reduce(lambda a, b: a + b, [t.astype(F32) for t in terms]).astype(BF16)


def shards(
    prefill_rows,
    decode_rows,
    norm_gain,
    w_query,
    w_key,
    w_value,
    w_out,
    prefix_keys,
    prefix_values,
    prefill_start,
    cache_keys,
    cache_values,
    cache_lengths,
):
    index = lax.axis_index("tensor")
    core, chip_x, chip_z = index & 1, (index >> 1) & 1, index >> 2
    rows = prefill_rows.shape[0]
    dec = decode_rows.shape[0]
    chips = 2 * RING
    half = rows // 2
    quarter = half // 2
    width = prefill_rows.shape[1]

    a0, b0 = norm_halves(prefill_rows, norm_gain)
    a1, b1 = side(a0), side(b0)
    a3, b3 = up(a0), up(b0)
    a2, b2 = down(a0), down(b0)
    dec_own = rms_norm(decode_rows, norm_gain)
    dec_rows = exchange(
        jnp.broadcast_to(dec_own[None], (chips, dec, width)).reshape(chips * dec, width)
    )
    wkv_own = jnp.concatenate([w_key.T, w_value.T], 0)
    wkv_other = swap(wkv_own)
    wq_other = swap(w_query)
    pkv_own = jnp.concatenate([prefix_keys.T, prefix_values.T], 0)
    pkv_other = swap(pkv_own)
    wo_other = swap(w_out)

    a6, b6 = up(a3), down(b2)
    a5, a4 = up(a1), down(a1)
    b4, b5 = side(b2), side(b3)
    a7 = [up(a5[:quarter]), down(a4[quarter:])]
    b7 = side(b6)

    low = jnp.where(core == 0, pkv_own, pkv_other)
    high = jnp.where(core == 0, pkv_other, pkv_own)
    kv_cols = prefix_keys.shape[1]
    prefix_k = jnp.concatenate([low[:kv_cols], high[:kv_cols]], 0).T
    prefix_v = jnp.concatenate([low[kv_cols:], high[kv_cols:]], 0).T

    places = []
    for z_off, flip in ((0, 0), (0, 1), (1, 0), (3, 0), (1, 1), (3, 1), (2, 0), (2, 1)):
        places.append((((chip_z + z_off) % RING) * 2 + (chip_x ^ flip)) * 2 + core)
    start = prefill_start[0]
    offsets = jnp.arange(rows, dtype=jnp.int32)
    near_pos = jnp.concatenate([start + p * rows + offsets for p in places[:4]])
    far_pos = jnp.concatenate([start + p * rows + offsets for p in places[4:]])
    near_cos, near_sin = tables(near_pos)
    far_cos, far_sin = tables(far_pos)
    core_spec = core.reshape(1).astype(jnp.int32)

    weights = (w_query, wq_other, wkv_own, wkv_other)
    turned = 4 * rows
    q_near, kv_near = project(
        [a0, b0, a1, b1, a2, b2, a3, b3, dec_rows],
        turned,
        core_spec,
        *weights,
        near_cos,
        near_sin,
        "project_near",
    )
    dec_qkv = jnp.concatenate([q_near[turned:], kv_near[turned:]], 1)
    q_near, kv_near = q_near[:turned], kv_near[:turned]
    kv_near_other = swap(kv_near)
    q_far, kv_far = project(
        [a4, b4, a5, b5, a6, b6, *a7, b7],
        turned,
        core_spec,
        *weights,
        far_cos,
        far_sin,
        "project_far",
    )
    kv_far_other = swap(kv_far)

    q_cols = 2 * w_query.shape[1]
    mine = exchange(dec_qkv).reshape(chips, dec, -1).transpose(1, 0, 2)
    dec_attn = decode_attend(
        mine[:, :, :q_cols].reshape(dec, chips, q_cols // HEAD_DIM, HEAD_DIM),
        mine[:, :, q_cols : q_cols + HEAD_DIM],
        mine[:, :, q_cols + HEAD_DIM :],
        cache_keys,
        cache_values,
        cache_lengths,
    )
    dec_attn = exchange(
        dec_attn.reshape(dec, chips, q_cols).transpose(1, 0, 2).reshape(chips * dec, q_cols)
    )

    own, other = [kv_near, kv_far], [kv_near_other, kv_far_other]
    head = [start] + places
    far_spec = jnp.stack(head + places[4:]).astype(jnp.int32)
    near_spec = jnp.stack(head + places[:4]).astype(jnp.int32)
    attn_far = attend(far_spec, q_far, prefix_k, prefix_v, own, other, rows, "attend_far")
    pieces = [half] * 6 + [quarter, quarter, half]
    p4a, p4b, p5a, p5b, p6a, p6b, p7lo, p7hi, p7b = emit(
        [attn_far], w_out, wo_other, pieces, "emit_far"
    )
    r6b = side(p7b)
    r4hi, r5lo = up(p7hi), down(p7lo)
    attn_near = attend(near_spec, q_near, prefix_k, prefix_v, own, other, rows, "attend_near")
    p0a, p0b, p1a, p1b, p2a, p2b, p3a, p3b, pdec = emit(
        [attn_near, dec_attn], w_out, wo_other, [half] * 8 + [chips * dec], "emit_near"
    )
    p4a = jnp.concatenate([p4a[:quarter], add(p4a[quarter:], r4hi)], 0)
    p5a = jnp.concatenate([add(p5a[:quarter], r5lo), p5a[quarter:]], 0)
    r1a_up, r1a_down = up(p4a), down(p5a)
    r2b_side, r3b_side = side(p4b), side(p5b)
    r3a = down(p6a)
    r2b = up(add(p6b, r6b))
    r0a_side = side(add(p1a, r1a_up, r1a_down))
    r0b_side = side(p1b)
    r0a_up, r0b_up = up(p2a), up(add(p2b, r2b_side, r2b))
    r0a_down, r0b_down = down(add(p3a, r3a)), down(add(p3b, r3b_side))
    prefill_out = jnp.concatenate(
        [add(p0a, r0a_side, r0a_up, r0a_down), add(p0b, r0b_side, r0b_up, r0b_down)], 0
    )
    dec_parts = exchange(pdec).reshape(chips, dec, width)
    decode_out = jnp.sum(dec_parts.astype(F32), axis=0).astype(BF16)
    return (prefill_out, decode_out)


def solution(mesh):
    in_specs = (
        P(("dp", "tensor"), None),
        P(("dp", "tensor"), None),
        P(),
        P(None, "tensor"),
        P(None, "tensor"),
        P(None, "tensor"),
        P("tensor", None),
        P("dp", "tensor"),
        P("dp", "tensor"),
        P("dp"),
        P(("dp", "tensor"), None, None),
        P(("dp", "tensor"), None, None),
        P(("dp", "tensor")),
    )
    out_specs = (P(("dp", "tensor"), None), P(("dp", "tensor"), None))
    return jax.shard_map(shards, mesh=mesh, in_specs=in_specs, out_specs=out_specs, check_vma=False)
```

time: 558 us -> 302 us (0.54)
  waiting for transfers between devices: 346 us -> 102 us
  matrix products: 100 us -> 2.25 us
  Pallas kernels: 0 us -> 68.2 us
  starting transfers between devices: 19.2 us -> 60.8 us
  between operations: 15.5 us -> 2.13 us
  local copies, waits for them, and re-layouts: 50.8 us -> 43.5 us
    reduce_scatter x1 -> x0, waiting for transfers between devices: 185 us -> none  [shards(): lax.psum_scatter(jnp.dot(attn_pre, w_out, preferred_element_type=jnp.floa...]
    all_gather x1 -> x0, waiting for transfers between devices: 101 us -> none  [shards(): project_normed = lax.all_gather(normed, 'tensor', axis=0, tiled=True)]
    ppermute x4 -> x36, waiting for transfers between devices: 0.01 us -> 95.5 us  [the longest x10 38.3 us: side(): return lax.ppermute(block, 'tensor', SIDE)]
    dot_general x9 -> x2, matrix products: 78.6 us -> 1.75 us  [the longest x1 1.55 us: decode_attend(): jnp.einsum('rgjd,rlgd->rgjl', q_rot, cache_k, preferred_element_type=F32)]
    pallas_call x0 -> x7, Pallas kernels: none -> 68.2 us  [the longest x2 23.4 us: attend(): pl.pallas_call(functools.partial(attend_kernel, blocks, prefix), grid_spe...]
    unnamed x4 -> x0, waiting for transfers between devices: 45.7 us -> none
    ppermute x4 -> x36, starting transfers between devices: 1.16 us -> 41.5 us  [the longest x10 18.6 us: down(): return lax.ppermute(block, 'tensor', DOWN)]
    sub x2 -> x0, matrix products: 20.9 us -> none  [attend_block(): weights = jnp.exp(scores - row_max)]
  transfers between devices with their start and end apart: 11 -> 40, of which waited for: 6 -> 15; matrix products, arithmetic and copies ran while one was open for 16% -> 10% of each run, Pallas kernels for 0% -> 19%
where the time goes in v1:
time: 302 us; the launch traced here: 299 us
  waiting for transfers between devices  102 us (34%)
  Pallas kernels  68.2 us (23%)
  starting transfers between devices  60.8 us (20%)
  local copies, waits for them, and re-layouts  43.5 us (14%)
  other arithmetic  20.9 us (7%)
    ppermute x10, waiting for transfers between devices, side(): return lax.ppermute(block, 'tensor', SIDE)  38.3 us
    ppermute x10, waiting for transfers between devices, down(): return lax.ppermute(block, 'tensor', DOWN)  38 us
    unnamed x122, local copies, waits for them, and re-layouts  32.7 us
    pallas_call x2, Pallas kernels, attend(): pl.pallas_call(functools.partial(attend_kernel, blocks, prefix), grid_spe...  23.4 us
    pallas_call x2, Pallas kernels, project(): pl.pallas_call(functools.partial(project_kernel, len(xs), turned), grid_s...  22.8 us
    pallas_call x2, Pallas kernels, emit(): pl.pallas_call(functools.partial(emit_kernel, len(xs), tuple(sizes)), gri...  19.5 us
    all_to_all x4, starting transfers between devices, exchange(): lax.all_to_all(block, 'tensor', split_axis=0, concat_axis=0, axis_index_g...  19.4 us
    ppermute x10, waiting for transfers between devices, up(): return lax.ppermute(block, 'tensor', UP)  19.1 us
  transfers between devices with their start and end apart: 40, of which 15 were waited for; matrix products, arithmetic and copies ran while one was open for 10% of the time, Pallas kernels for 19%

profile of v1, /device:TPU:0, one launch (start us, length us, event | category | flops | bytes accessed | tf_op | source)
XLA Modules:
  0.0 299.3 jit_solution(399147354948445835)
XLA Ops:
  0.8 1.5 reshape.243.gain_ref
  2.3 2.5 norm_halves.1
  4.8 1.6 collective-permute-start
  6.4 1.9 collective-permute-start.4
  11.2 4.9 %all-to-all-start = ((bf16[8,2,8192]{2,1,0:T(2,128)(2,1)}), bf16[8,2,8192]{2,1,0:T(2,128)(2,1)}, u32[]{:S(2)}, u32[]{:S(2)}) async-start(bf16[8,2,8192]{2,1,0:T(2,128)(2,1)} %broadcast_in_dim.10), calls=%async_computation | async-start | bytes 524288 | tf_op jit(solution)/shard_map/all_to_all | solution.py:52
  16.1 3.3 %collective-permute-start.3 = (bf16[32,8192]{1,0:T(8,128)(2,1)S(1)}, bf16[32,8192]{1,0:T(8,128)(2,1)}, u32[]{:S(2)}, u32[]{:S(2)}) collective-permute-start(bf16[32,8192]{1,0:T(8,128)(2,1)S(1)} %copy-done.15), channel_id=1, source_target_pairs={{0,12},{1,13},{2,14},{3,15},{4,0},{5,1},{6,2},{7,3},{8,4},{9,5},{1... | collective-permute-start | bytes 1572872 | tf_op jit(solution)/shard_map/ppermute | solution.py:40
  19.4 3.1 %pad_maximum_fusion.refs_11_ = bf16[128,8192]{1,0:T(8,128)(2,1)} fusion(bf16[64,8192]{1,0:T(8,128)(2,1)} %bitcast.71, bf16[64,8192]{1,0:T(8,128)(2,1)} %bitcast.72), kind=kLoop, calls=%fused_computation.6 | loop fusion | flops 4194304 | bytes 4194304 | tf_op jit(solution)/shard_map/concatenate | solution.py:381
  23.3 9.4 %collective-permute-done.3.refs_5_ = bf16[32,8192]{1,0:T(8,128)(2,1)} collective-permute-done((bf16[32,8192]{1,0:T(8,128)(2,1)S(1)}, bf16[32,8192]{1,0:T(8,128)(2,1)}, u32[]{:S(2)}, u32[]{:S(2)}) %collective-permute-start.3) | collective-permute-done | bytes 524320 | tf_op jit(solution)/shard_map/ppermute | solution.py:40
  32.7 1.5 collective-permute-start.1
  34.5 3.7 %collective-permute-done.5.refs_7_ = bf16[32,8192]{1,0:T(8,128)(2,1)S(1)} collective-permute-done((bf16[32,8192]{1,0:T(8,128)(2,1)S(1)}, bf16[32,8192]{1,0:T(8,128)(2,1)S(1)}, u32[]{:S(2)}, u32[]{:S(2)}) %collective-permute-start.5) | collective-permute-done | bytes 524320 | tf_op jit(solution)/shard_map/ppermute | solution.py:36
  38.6 7.0 %collective-permute-done.1.refs_3_ = bf16[32,8192]{1,0:T(8,128)(2,1)S(1)} collective-permute-done((bf16[32,8192]{1,0:T(8,128)(2,1)S(1)}, bf16[32,8192]{1,0:T(8,128)(2,1)S(1)}, u32[]{:S(2)}, u32[]{:S(2)}) %collective-permute-start.1) | collective-permute-done | bytes 524320 | tf_op jit(solution)/shard_map/ppermute | solution.py:44
  51.7 1.9 collective-permute-start.9
  53.7 6.9 %collective-permute-done.11.refs_2_ = bf16[32,8192]{1,0:T(8,128)(2,1)S(1)} collective-permute-done((bf16[32,8192]{1,0:T(8,128)(2,1)}, bf16[32,8192]{1,0:T(8,128)(2,1)S(1)}, u32[]{:S(2)}, u32[]{:S(2)}) %collective-permute-start.11) | collective-permute-done | bytes 524320 | tf_op jit(solution)/shard_map/ppermute | solution.py:36
  60.6 1.7 collective-permute-start.14
  64.4 1.9 collective-permute-done.9.refs_0_
  67.7 7.6 %collective-permute-done.14.refs_5_ = bf16[32,8192]{1,0:T(8,128)(2,1)} collective-permute-done((bf16[32,8192]{1,0:T(8,128)(2,1)}, bf16[32,8192]{1,0:T(8,128)(2,1)}, u32[]{:S(2)}, u32[]{:S(2)}) %collective-permute-start.14) | collective-permute-done | bytes 524320 | tf_op jit(solution)/shard_map/ppermute | solution.py:40
  82.8 4.6 %collective-permute-done.12.refs_3_ = bf16[32,8192]{1,0:T(8,128)(2,1)S(1)} collective-permute-done((bf16[32,8192]{1,0:T(8,128)(2,1)}, bf16[32,8192]{1,0:T(8,128)(2,1)S(1)}, u32[]{:S(2)}, u32[]{:S(2)}) %collective-permute-start.12) | collective-permute-done | bytes 524320 | tf_op jit(solution)/shard_map/ppermute | solution.py:44
  88.2 1.6 collective-permute-start.15
  89.9 1.6 collective-permute-start.16
  92.4 3.4 %copy-done.2 = bf16[8192,512]{1,0:T(8,128)(2,1)S(1)} copy-done((bf16[8192,512]{1,0:T(8,128)(2,1)S(1)}, bf16[8192,512]{1,0:T(8,128)(2,1)}, u32[]{:S(2)}) %copy-start.2) | copy-done | bytes 8388632
  95.8 11.1 %project_near.1 = (bf16[272,1024]{1,0:T(8,128)(2,1)S(1)}, bf16[272,256]{1,0:T(8,128)(2,1)S(1)}) custom-call(s32[1]{0:T(128)} %bitcast.8.core_ref, bf16[32,8192]{1,0:T(8,128)(2,1)S(1)} %copy-done.14, bf16[32,8192]{1,0:T(8,128)(2,1)S(1)} %copy-done.16, bf16[32,8192]{1,0:T(8,128)(2,1)} %collective-permute-done.refs_2_, bf16[32,8192]{1,0:T(8,128)(2,1)S(1)} %copy-done.20, ...), custom_call_target="tpu_custom_call" | custom-call | flops 5704253440 | bytes 25427968 | tf_op jit(solution)/shard_map/project_near/pallas_call | solution.py:136
  108.3 4.0 %all-to-all-start.1 = ((bf16[8,2,1280]{2,1,0:T(2,128)(2,1)}), bf16[8,2,1280]{2,1,0:T(2,128)(2,1)S(1)}, u32[]{:S(2)}, u32[]{:S(2)}) async-start(bf16[8,2,1280]{2,1,0:T(2,128)(2,1)} %all_to_all.24), calls=%async_computation.1 | async-start | bytes 81920 | tf_op jit(solution)/shard_map/all_to_all | solution.py:52
  112.6 3.4 %copy-done.3 = bf16[8192,512]{1,0:T(8,128)(2,1)S(1)} copy-done((bf16[8192,512]{1,0:T(8,128)(2,1)S(1)}, bf16[8192,512]{1,0:T(8,128)(2,1)}, u32[]{:S(2)}) %copy-start.3) | copy-done | bytes 8388632
  116.0 1.6 copy-done.7
  120.5 11.7 %project_far.1 = (bf16[256,1024]{1,0:T(8,128)(2,1)S(1)}, bf16[256,256]{1,0:T(8,128)(2,1)}) custom-call(s32[1]{0:T(128)} %bitcast.8.core_ref, bf16[32,8192]{1,0:T(8,128)(2,1)S(1)} %collective-permute-done.9.refs_0_, bf16[32,8192]{1,0:T(8,128)(2,1)S(1)} %copy-done.24, bf16[32,8192]{1,0:T(8,128)(2,1)S(1)} %collective-permute-done.11.refs_2_, ...), custom_call_target="tpu_custom_call" | custom-call | flops 5368709120 | bytes 25165824 | tf_op jit(solution)/shard_map/project_far/pallas_call | solution.py:136
  134.1 1.6 fusion.36
  137.1 5.4 %all-to-all-start.2 = ((bf16[8,2,1024]{2,1,0:T(2,128)(2,1)}), bf16[8,2,1024]{2,1,0:T(2,128)(2,1)S(1)}, u32[]{:S(2)}, u32[]{:S(2)}) async-start(bf16[8,2,1024]{2,1,0:T(2,128)(2,1)} %bitcast.58), calls=%async_computation.2 | async-start | bytes 65536 | tf_op jit(solution)/shard_map/all_to_all | solution.py:52
  142.8 6.0 %all-to-all-done.2 = bf16[8,2,1024]{2,1,0:T(2,128)(2,1)S(1)} async-done(((bf16[8,2,1024]{2,1,0:T(2,128)(2,1)}), bf16[8,2,1024]{2,1,0:T(2,128)(2,1)S(1)}, u32[]{:S(2)}, u32[]{:S(2)}) %all-to-all-start.2) | async-done | bytes 32800 | tf_op jit(solution)/shard_map/all_to_all | solution.py:52
  148.9 12.2 %attend_far.1.refs_0_ = bf16[256,1024]{1,0:T(8,128)(2,1)S(1)} custom-call(s32[13]{0:T(128)S(1)} %stack.55.spec_ref, bf16[256,1024]{1,0:T(8,128)(2,1)S(1)} %copy-done.44, bf16[1024,128]{1,0:T(8,128)(2,1)S(1)} %copy-done.37, bf16[1024,128]{1,0:T(8,128)(2,1)S(1)} %maximum_bitcast_fusion.1.pv_ref, bf16[256,256]{1,0:T(8,128)(2,1)S(1)} %slice.68.refs_0_, ...), custom_call_target="tpu_custom_call" | custom-call | flops 2147483648 | bytes 2621440 | tf_op jit(solution)/shard_map/attend_far/pallas_call | solution.py:234
  161.1 3.4 %copy-done.4 = bf16[512,8192]{1,0:T(8,128)(2,1)S(1)} copy-done((bf16[512,8192]{1,0:T(8,128)(2,1)S(1)}, bf16[512,8192]{1,0:T(8,128)(2,1)}, u32[]{:S(2)}) %copy-start.4) | copy-done | bytes 8388632
  164.5 9.9 %emit_far.1 = (bf16[32,8192]{1,0:T(8,128)(2,1)S(1)}, bf16[32,8192]{1,0:T(8,128)(2,1)S(1)}, bf16[32,8192]{1,0:T(8,128)(2,1)S(1)}, bf16[32,8192]{1,0:T(8,128)(2,1)...) custom-call(bf16[256,1024]{1,0:T(8,128)(2,1)S(1)} %attend_far.1.refs, ...), custom_call_target="tpu_custom_call" | custom-call | flops 4294967296 | bytes 21495808 | tf_op jit(solution)/shard_map/emit_far/pallas_call | solution.py:280
  180.5 11.2 %attend_near.1.refs_0_ = bf16[256,1024]{1,0:T(8,128)(2,1)S(1)} custom-call(s32[13]{0:T(128)S(1)} %stack.54.spec_ref, bf16[256,1024]{1,0:T(8,128)(2,1)S(1)} %slice.63.q_ref, bf16[1024,128]{1,0:T(8,128)(2,1)S(1)} %copy-done.37, bf16[1024,128]{1,0:T(8,128)(2,1)S(1)} %maximum_bitcast_fusion.1.pv_ref, bf16[256,256]{1,0:T(8,128)(2,1)S(1)} %slice.68.refs_0_, ...), custom_call_target="tpu_custom_call" | custom-call | flops 2147483648 | bytes 2621440 | tf_op jit(solution)/shard_map/attend_near/pallas_call | solution.py:234
  191.7 3.4 %copy-done.5 = bf16[512,8192]{1,0:T(8,128)(2,1)S(1)} copy-done((bf16[512,8192]{1,0:T(8,128)(2,1)S(1)}, bf16[512,8192]{1,0:T(8,128)(2,1)}, u32[]{:S(2)}) %copy-start.5) | copy-done | bytes 8388632
  195.1 9.5 %emit_near.1 = (bf16[32,8192]{1,0:T(8,128)(2,1)S(1)}, bf16[32,8192]{1,0:T(8,128)(2,1)S(1)}, bf16[32,8192]{1,0:T(8,128)(2,1)S(1)}, bf16[32,8192]{1,0:T(8,128)(2,1...) custom-call(bf16[256,1024]{1,0:T(8,128)(2,1)S(1)} %attend_near.1.ref, ...), custom_call_target="tpu_custom_call" | custom-call | flops 4563402752 | bytes 21790720 | tf_op jit(solution)/shard_map/emit_near/pallas_call | solution.py:280
  209.6 5.1 %all-to-all-start.3 = ((bf16[8,2,8192]{2,1,0:T(2,128)(2,1)}), bf16[8,2,8192]{2,1,0:T(2,128)(2,1)S(1)}, u32[]{:S(2)}, u32[]{:S(2)}) async-start(bf16[8,2,8192]{2,1,0:T(2,128)(2,1)} %all_to_all.28), calls=%async_computation.3 | async-start | bytes 524288 | tf_op jit(solution)/shard_map/all_to_all | solution.py:52
  214.7 1.7 slice.80
  216.3 3.2 %collective-permute-start.23 = (bf16[16,8192]{1,0:T(8,128)(2,1)}, bf16[16,8192]{1,0:T(8,128)(2,1)}, u32[]{:S(2)}, u32[]{:S(2)}) collective-permute-start(bf16[16,8192]{1,0:T(8,128)(2,1)} %copy-done.47), channel_id=1, source_target_pairs={{0,12},{1,13},{2,14},{3,15},{4,0},{5,1},{6,2},{7,3},{8,4},{9,5},{1... | collective-permute-start | bytes 786440 | tf_op jit(solution)/shard_map/ppermute | solution.py:40
  222.3 1.5 collective-permute-start.31
  227.3 1.5 collective-permute-start.34
  229.9 5.9 %collective-permute-done.27 = bf16[32,8192]{1,0:T(8,128)(2,1)} collective-permute-done((bf16[32,8192]{1,0:T(8,128)(2,1)}, bf16[32,8192]{1,0:T(8,128)(2,1)}, u32[]{:S(2)}, u32[]{:S(2)}) %collective-permute-start.27) | collective-permute-done | bytes 524320 | tf_op jit(solution)/shard_map/ppermute | solution.py:40
  235.8 1.5 collective-permute-start.29
  238.5 1.6 collective-permute-start.22
  241.3 18.6 %collective-permute-done.34 = bf16[32,8192]{1,0:T(8,128)(2,1)S(1)} collective-permute-done((bf16[32,8192]{1,0:T(8,128)(2,1)}, bf16[32,8192]{1,0:T(8,128)(2,1)S(1)}, u32[]{:S(2)}, u32[]{:S(2)}) %collective-permute-start.34) | collective-permute-done | bytes 524320 | tf_op jit(solution)/shard_map/ppermute | solution.py:44
  259.9 2.1 collective-permute-start.24
  262.1 12.6 %collective-permute-done.24 = bf16[32,8192]{1,0:T(8,128)(2,1)S(1)} collective-permute-done((bf16[32,8192]{1,0:T(8,128)(2,1)S(1)}, bf16[32,8192]{1,0:T(8,128)(2,1)S(1)}, u32[]{:S(2)}, u32[]{:S(2)}) %collective-permute-start.24) | collective-permute-done | bytes 524320 | tf_op jit(solution)/shard_map/ppermute | solution.py:40
  274.9 3.3 %collective-permute-start.35 = (bf16[32,8192]{1,0:T(8,128)(2,1)S(1)}, bf16[32,8192]{1,0:T(8,128)(2,1)S(1)}, u32[]{:S(2)}, u32[]{:S(2)}) collective-permute-start(bf16[32,8192]{1,0:T(8,128)(2,1)S(1)} %add_convert_fusion.1), channel_id=1, source_target_pairs={{0,12},{1,13},{2,14},{3,15},{4,0},{5,1},{6,2},{7,3},{8,4},{9,5},{1... | collective-permute-start | bytes 1572872 | tf_op jit(solution)/shard_map/ppermute | solution.py:40
  278.3 7.6 %collective-permute-done.32 = bf16[32,8192]{1,0:T(8,128)(2,1)S(1)} collective-permute-done((bf16[32,8192]{1,0:T(8,128)(2,1)S(1)}, bf16[32,8192]{1,0:T(8,128)(2,1)S(1)}, u32[]{:S(2)}, u32[]{:S(2)}) %collective-permute-start.32) | collective-permute-done | bytes 524320 | tf_op jit(solution)/shard_map/ppermute | solution.py:36
  286.9 8.1 %collective-permute-done.25 = bf16[32,8192]{1,0:T(8,128)(2,1)S(1)} collective-permute-done((bf16[32,8192]{1,0:T(8,128)(2,1)S(1)}, bf16[32,8192]{1,0:T(8,128)(2,1)S(1)}, u32[]{:S(2)}, u32[]{:S(2)}) %collective-permute-start.25) | collective-permute-done | bytes 524320 | tf_op jit(solution)/shard_map/ppermute | solution.py:44
  (231 shorter events, 56.9 us)
Async XLA Ops:
  0.6 133.4 %copy-start = (bf16[2,512,1024]{2,1,0:T(8,128)(2,1)S(1)}, bf16[2,512,1024]{2,1,0:T(8,128)(2,1)}, u32[]{:S(2)}) copy-start(bf16[2,512,1024]{2,1,0:T(8,128)(2,1)} %param.23) | copy-start | bytes 6291460
  0.7 90.8 %collective-permute-start.6 = (bf16[8192,512]{1,0:T(8,128)(2,1)}, bf16[8192,512]{1,0:T(8,128)(2,1)}, u32[]{:S(2)}, u32[]{:S(2)}) collective-permute-start(bf16[8192,512]{1,0:T(8,128)(2,1)} %refs_9_.3), channel_id=1, source_target_pairs={{0,1},{1,0},{2,3},{3,2},{4,5},{5,4},{6,7},{7,6},{8,9},{9,8},{10,11... | collective-permute-start | bytes 25165832 | tf_op jit(solution)/shard_map/ppermute | solution.py:48
  4.8 18.4 %collective-permute-start = (bf16[32,8192]{1,0:T(8,128)(2,1)}, bf16[32,8192]{1,0:T(8,128)(2,1)}, u32[]{:S(2)}, u32[]{:S(2)}) collective-permute-start(bf16[32,8192]{1,0:T(8,128)(2,1)} %get-tuple-element.26.refs_0_), channel_id=1, source_target_pairs={{0,2},{1,3},{2,0},{3,1},{4,6},{5,7},{6,4},{7,5},{8,10},{9,11},{10,... | collective-permute-start | bytes 1572872 | tf_op jit(solution)/shard_map/ppermute | solution.py:44
  6.4 27.8 %collective-permute-start.4 = (bf16[32,8192]{1,0:T(8,128)(2,1)}, bf16[32,8192]{1,0:T(8,128)(2,1)}, u32[]{:S(2)}, u32[]{:S(2)}) collective-permute-start(bf16[32,8192]{1,0:T(8,128)(2,1)} %get-tuple-element.26.refs_0_), channel_id=1, source_target_pairs={{0,4},{1,5},{2,6},{3,7},{4,8},{5,9},{6,10},{7,11},{8,12},{9,13},{1... | collective-permute-start | bytes 1572872 | tf_op jit(solution)/shard_map/ppermute | solution.py:36
  9.5 6.5 %collective-permute-start.8 = (bf16[128,1024]{0,1:T(8,128)(2,1)}, bf16[128,1024]{0,1:T(8,128)(2,1)S(1)}, u32[]{:S(2)}, u32[]{:S(2)}) collective-permute-start(bf16[128,1024]{0,1:T(8,128)(2,1)} %pad_maximum_fusion.4), channel_id=1, source_target_pairs={{0,1},{1,0},{2,3},{3,2},{4,5},{5,4},{6,7},{7,6},{8,9},{9,8},{10,11... | collective-permute-start | bytes 786440 | tf_op jit(solution)/shard_map/ppermute | solution.py:48
  9.5 151.6 %collective-permute-start.20 = (bf16[512,8192]{1,0:T(8,128)(2,1)}, bf16[512,8192]{1,0:T(8,128)(2,1)}, u32[]{:S(2)}, u32[]{:S(2)}) collective-permute-start(bf16[512,8192]{1,0:T(8,128)(2,1)} %refs_1_.1), channel_id=1, source_target_pairs={{0,1},{1,0},{2,3},{3,2},{4,5},{5,4},{6,7},{7,6},{8,9},{9,8},{10,11... | collective-permute-start | bytes 25165832 | tf_op jit(solution)/shard_map/ppermute | solution.py:48
  11.2 52.2 %all-to-all-start = ((bf16[8,2,8192]{2,1,0:T(2,128)(2,1)}), bf16[8,2,8192]{2,1,0:T(2,128)(2,1)}, u32[]{:S(2)}, u32[]{:S(2)}) async-start(bf16[8,2,8192]{2,1,0:T(2,128)(2,1)} %broadcast_in_dim.10), calls=%async_computation | async-start | bytes 524288 | tf_op jit(solution)/shard_map/all_to_all | solution.py:52
  16.1 16.7 %collective-permute-start.3 = (bf16[32,8192]{1,0:T(8,128)(2,1)S(1)}, bf16[32,8192]{1,0:T(8,128)(2,1)}, u32[]{:S(2)}, u32[]{:S(2)}) collective-permute-start(bf16[32,8192]{1,0:T(8,128)(2,1)S(1)} %copy-done.15), channel_id=1, source_target_pairs={{0,12},{1,13},{2,14},{3,15},{4,0},{5,1},{6,2},{7,3},{8,4},{9,5},{1... | collective-permute-start | bytes 1572872 | tf_op jit(solution)/shard_map/ppermute | solution.py:40
  19.4 18.8 %copy-start.13 = (bf16[32,8192]{1,0:T(8,128)(2,1)S(1)}, bf16[32,8192]{1,0:T(8,128)(2,1)}, u32[]{:S(2)}) copy-start(bf16[32,8192]{1,0:T(8,128)(2,1)} %get-tuple-element.26.refs_0_) | copy-start | bytes 1572868
  19.4 42.9 %copy-start.58 = (s32[2]{0:T(128)S(1)}, s32[2]{0:T(128)}, u32[]{:S(2)}) copy-start(s32[2]{0:T(128)} %param.25) | copy-start | bytes 28
  23.2 15.0 %collective-permute-start.5 = (bf16[32,8192]{1,0:T(8,128)(2,1)S(1)}, bf16[32,8192]{1,0:T(8,128)(2,1)S(1)}, u32[]{:S(2)}, u32[]{:S(2)}) collective-permute-start(bf16[32,8192]{1,0:T(8,128)(2,1)S(1)} %copy-done.15), channel_id=1, source_target_pairs={{0,4},{1,5},{2,6},{3,7},{4,8},{5,9},{6,10},{7,11},{8,12},{9,13},{1... | collective-permute-start | bytes 1572872 | tf_op jit(solution)/shard_map/ppermute | solution.py:36
  32.7 12.9 %collective-permute-start.1 = (bf16[32,8192]{1,0:T(8,128)(2,1)S(1)}, bf16[32,8192]{1,0:T(8,128)(2,1)S(1)}, u32[]{:S(2)}, u32[]{:S(2)}) collective-permute-start(bf16[32,8192]{1,0:T(8,128)(2,1)S(1)} %copy-done.15), channel_id=1, source_target_pairs={{0,2},{1,3},{2,0},{3,1},{4,6},{5,7},{6,4},{7,5},{8,10},{9,11},{10,... | collective-permute-start | bytes 1572872 | tf_op jit(solution)/shard_map/ppermute | solution.py:44
  34.2 55.7 %collective-permute-start.7 = (bf16[128,8192]{1,0:T(8,128)(2,1)}, bf16[128,8192]{1,0:T(8,128)(2,1)}, u32[]{:S(2)}, u32[]{:S(2)}) collective-permute-start(bf16[128,8192]{1,0:T(8,128)(2,1)} %pad_maximum_fusion.refs_11_), channel_id=1, source_target_pairs={{0,1},{1,0},{2,3},{3,2},{4,5},{5,4},{6,7},{7,6},{8,9},{9,8},{10,11... | collective-permute-start | bytes 6291464 | tf_op jit(solution)/shard_map/ppermute | solution.py:48
  38.2 24.8 %copy-start.17 = (bf16[32,8192]{1,0:T(8,128)(2,1)}, bf16[32,8192]{1,0:T(8,128)(2,1)S(1)}, u32[]{:S(2)}) copy-start(bf16[32,8192]{1,0:T(8,128)(2,1)S(1)} %collective-permute-done.5.refs_7_) | copy-start | bytes 1572868
  38.2 12.7 %collective-permute-start.2 = (bf16[32,8192]{1,0:T(8,128)(2,1)S(1)}, bf16[32,8192]{1,0:T(8,128)(2,1)S(1)}, u32[]{:S(2)}, u32[]{:S(2)}) collective-permute-start(bf16[32,8192]{1,0:T(8,128)(2,1)S(1)} %copy-done.13), channel_id=1, source_target_pairs={{0,12},{1,13},{2,14},{3,15},{4,0},{5,1},{6,2},{7,3},{8,4},{9,5},{1... | collective-permute-start | bytes 1572872 | tf_op jit(solution)/shard_map/ppermute | solution.py:40
  45.6 14.9 %collective-permute-start.11 = (bf16[32,8192]{1,0:T(8,128)(2,1)}, bf16[32,8192]{1,0:T(8,128)(2,1)S(1)}, u32[]{:S(2)}, u32[]{:S(2)}) collective-permute-start(bf16[32,8192]{1,0:T(8,128)(2,1)} %collective-permute-done.refs_2_), channel_id=1, source_target_pairs={{0,4},{1,5},{2,6},{3,7},{4,8},{5,9},{6,10},{7,11},{8,12},{9,13},{1... | collective-permute-start | bytes 1572872 | tf_op jit(solution)/shard_map/ppermute | solution.py:36
  51.7 14.6 %collective-permute-start.9 = (bf16[32,8192]{1,0:T(8,128)(2,1)}, bf16[32,8192]{1,0:T(8,128)(2,1)S(1)}, u32[]{:S(2)}, u32[]{:S(2)}) collective-permute-start(bf16[32,8192]{1,0:T(8,128)(2,1)} %collective-permute-done.refs_2_), channel_id=1, source_target_pairs={{0,12},{1,13},{2,14},{3,15},{4,0},{5,1},{6,2},{7,3},{8,4},{9,5},{1... | collective-permute-start | bytes 1572872 | tf_op jit(solution)/shard_map/ppermute | solution.py:40
  60.6 14.7 %collective-permute-start.14 = (bf16[32,8192]{1,0:T(8,128)(2,1)}, bf16[32,8192]{1,0:T(8,128)(2,1)}, u32[]{:S(2)}, u32[]{:S(2)}) collective-permute-start(bf16[32,8192]{1,0:T(8,128)(2,1)} %collective-permute-done.3.refs_5_), channel_id=1, source_target_pairs={{0,12},{1,13},{2,14},{3,15},{4,0},{5,1},{6,2},{7,3},{8,4},{9,5},{1... | collective-permute-start | bytes 1572872 | tf_op jit(solution)/shard_map/ppermute | solution.py:40
  66.4 14.4 %collective-permute-start.10 = (bf16[32,8192]{1,0:T(8,128)(2,1)}, bf16[32,8192]{1,0:T(8,128)(2,1)S(1)}, u32[]{:S(2)}, u32[]{:S(2)}) collective-permute-start(bf16[32,8192]{1,0:T(8,128)(2,1)} %collective-permute-done.3.refs_5_), channel_id=1, source_target_pairs={{0,2},{1,3},{2,0},{3,1},{4,6},{5,7},{6,4},{7,5},{8,10},{9,11},{10,... | collective-permute-start | bytes 1572872 | tf_op jit(solution)/shard_map/ppermute | solution.py:44
  75.2 12.2 %collective-permute-start.12 = (bf16[32,8192]{1,0:T(8,128)(2,1)}, bf16[32,8192]{1,0:T(8,128)(2,1)S(1)}, u32[]{:S(2)}, u32[]{:S(2)}) collective-permute-start(bf16[32,8192]{1,0:T(8,128)(2,1)} %copy-done.17), channel_id=1, source_target_pairs={{0,2},{1,3},{2,0},{3,1},{4,6},{5,7},{6,4},{7,5},{8,10},{9,11},{10,... | collective-permute-start | bytes 1572872 | tf_op jit(solution)/shard_map/ppermute | solution.py:44
  81.5 30.7 %collective-permute-start.13 = (bf16[32,8192]{1,0:T(8,128)(2,1)}, bf16[32,8192]{1,0:T(8,128)(2,1)}, u32[]{:S(2)}, u32[]{:S(2)}) collective-permute-start(bf16[32,8192]{1,0:T(8,128)(2,1)} %collective-permute-done.4.refs_6_), channel_id=1, source_target_pairs={{0,4},{1,5},{2,6},{3,7},{4,8},{5,9},{6,10},{7,11},{8,12},{9,13},{1... | collective-permute-start | bytes 1572872 | tf_op jit(solution)/shard_map/ppermute | solution.py:36
  88.2 24.3 %collective-permute-start.15 = (bf16[16,8192]{1,0:T(8,128)(2,1)}, bf16[16,8192]{1,0:T(8,128)(2,1)}, u32[]{:S(2)}, u32[]{:S(2)}) collective-permute-start(bf16[16,8192]{1,0:T(8,128)(2,1)} %slice.88), channel_id=1, source_target_pairs={{0,4},{1,5},{2,6},{3,7},{4,8},{5,9},{6,10},{7,11},{8,12},{9,13},{1... | collective-permute-start | bytes 786440 | tf_op jit(solution)/shard_map/ppermute | solution.py:36
  89.9 22.7 %collective-permute-start.16 = (bf16[16,8192]{1,0:T(8,128)(2,1)}, bf16[16,8192]{1,0:T(8,128)(2,1)}, u32[]{:S(2)}, u32[]{:S(2)}) collective-permute-start(bf16[16,8192]{1,0:T(8,128)(2,1)} %slice.89), channel_id=1, source_target_pairs={{0,12},{1,13},{2,14},{3,15},{4,0},{5,1},{6,2},{7,3},{8,4},{9,5},{1... | collective-permute-start | bytes 786440 | tf_op jit(solution)/shard_map/ppermute | solution.py:40
  91.5 21.0 %collective-permute-start.17 = (bf16[32,8192]{1,0:T(8,128)(2,1)}, bf16[32,8192]{1,0:T(8,128)(2,1)}, u32[]{:S(2)}, u32[]{:S(2)}) collective-permute-start(bf16[32,8192]{1,0:T(8,128)(2,1)} %collective-permute-done.14.refs_5_), channel_id=1, source_target_pairs={{0,2},{1,3},{2,0},{3,1},{4,6},{5,7},{6,4},{7,5},{8,10},{9,11},{10,... | collective-permute-start | bytes 1572872 | tf_op jit(solution)/shard_map/ppermute | solution.py:44
  108.3 25.3 %all-to-all-start.1 = ((bf16[8,2,1280]{2,1,0:T(2,128)(2,1)}), bf16[8,2,1280]{2,1,0:T(2,128)(2,1)S(1)}, u32[]{:S(2)}, u32[]{:S(2)}) async-start(bf16[8,2,1280]{2,1,0:T(2,128)(2,1)} %all_to_all.24), calls=%async_computation.1 | async-start | bytes 81920 | tf_op jit(solution)/shard_map/all_to_all | solution.py:52
  112.3 36.6 %collective-permute-start.18 = (bf16[256,256]{1,0:T(8,128)(2,1)S(1)}, bf16[256,256]{1,0:T(8,128)(2,1)}, u32[]{:S(2)}, u32[]{:S(2)}) collective-permute-start(bf16[256,256]{1,0:T(8,128)(2,1)S(1)} %slice.68.refs_0_), channel_id=1, source_target_pairs={{0,1},{1,0},{2,3},{3,2},{4,5},{5,4},{6,7},{7,6},{8,9},{9,8},{10,11... | collective-permute-start | bytes 393224 | tf_op jit(solution)/shard_map/ppermute | solution.py:48
  133.1 15.8 %collective-permute-start.19 = (bf16[256,256]{1,0:T(8,128)(2,1)}, bf16[256,256]{1,0:T(8,128)(2,1)S(1)}, u32[]{:S(2)}, u32[]{:S(2)}) collective-permute-start(bf16[256,256]{1,0:T(8,128)(2,1)} %get-tuple-element.30.refs_1_), channel_id=1, source_target_pairs={{0,1},{1,0},{2,3},{3,2},{4,5},{5,4},{6,7},{7,6},{8,9},{9,8},{10,11... | collective-permute-start | bytes 393224 | tf_op jit(solution)/shard_map/ppermute | solution.py:48
  137.1 11.7 %all-to-all-start.2 = ((bf16[8,2,1024]{2,1,0:T(2,128)(2,1)}), bf16[8,2,1024]{2,1,0:T(2,128)(2,1)S(1)}, u32[]{:S(2)}, u32[]{:S(2)}) async-start(bf16[8,2,1024]{2,1,0:T(2,128)(2,1)} %bitcast.58), calls=%async_computation.2 | async-start | bytes 65536 | tf_op jit(solution)/shard_map/all_to_all | solution.py:52
  179.9 44.7 %collective-permute-start.21 = (bf16[16,8192]{1,0:T(8,128)(2,1)}, bf16[16,8192]{1,0:T(8,128)(2,1)}, u32[]{:S(2)}, u32[]{:S(2)}) collective-permute-start(bf16[16,8192]{1,0:T(8,128)(2,1)} %get-tuple-element.35), channel_id=1, source_target_pairs={{0,4},{1,5},{2,6},{3,7},{4,8},{5,9},{6,10},{7,11},{8,12},{9,13},{1... | collective-permute-start | bytes 786440 | tf_op jit(solution)/shard_map/ppermute | solution.py:36
  195.1 24.5 %copy-start.30 = (bf16[32,8192]{1,0:T(8,128)(2,1)S(1)}, bf16[32,8192]{1,0:T(8,128)(2,1)}, u32[]{:S(2)}) copy-start(bf16[32,8192]{1,0:T(8,128)(2,1)} %copy-done.29) | copy-start | bytes 1572868
  208.6 20.2 %copy-start.31 = (bf16[32,8192]{1,0:T(8,128)(2,1)S(1)}, bf16[32,8192]{1,0:T(8,128)(2,1)}, u32[]{:S(2)}) copy-start(bf16[32,8192]{1,0:T(8,128)(2,1)} %copy-done.29) | copy-start | bytes 1572868
  209.6 14.2 %all-to-all-start.3 = ((bf16[8,2,8192]{2,1,0:T(2,128)(2,1)}), bf16[8,2,8192]{2,1,0:T(2,128)(2,1)S(1)}, u32[]{:S(2)}, u32[]{:S(2)}) async-start(bf16[8,2,8192]{2,1,0:T(2,128)(2,1)} %all_to_all.28), calls=%async_computation.3 | async-start | bytes 524288 | tf_op jit(solution)/shard_map/all_to_all | solution.py:52
  216.3 11.0 %collective-permute-start.23 = (bf16[16,8192]{1,0:T(8,128)(2,1)}, bf16[16,8192]{1,0:T(8,128)(2,1)}, u32[]{:S(2)}, u32[]{:S(2)}) collective-permute-start(bf16[16,8192]{1,0:T(8,128)(2,1)} %copy-done.47), channel_id=1, source_target_pairs={{0,12},{1,13},{2,14},{3,15},{4,0},{5,1},{6,2},{7,3},{8,4},{9,5},{1... | collective-permute-start | bytes 786440 | tf_op jit(solution)/shard_map/ppermute | solution.py:40
  220.3 15.5 %collective-permute-start.27 = (bf16[32,8192]{1,0:T(8,128)(2,1)}, bf16[32,8192]{1,0:T(8,128)(2,1)}, u32[]{:S(2)}, u32[]{:S(2)}) collective-permute-start(bf16[32,8192]{1,0:T(8,128)(2,1)} %copy-done.46), channel_id=1, source_target_pairs={{0,12},{1,13},{2,14},{3,15},{4,0},{5,1},{6,2},{7,3},{8,4},{9,5},{1... | collective-permute-start | bytes 1572872 | tf_op jit(solution)/shard_map/ppermute | solution.py:40
  221.1 65.7 %collective-permute-start.26 = (bf16[32,8192]{1,0:T(8,128)(2,1)}, bf16[32,8192]{1,0:T(8,128)(2,1)}, u32[]{:S(2)}, u32[]{:S(2)}) collective-permute-start(bf16[32,8192]{1,0:T(8,128)(2,1)} %copy-done.41), channel_id=1, source_target_pairs={{0,4},{1,5},{2,6},{3,7},{4,8},{5,9},{6,10},{7,11},{8,12},{9,13},{1... | collective-permute-start | bytes 1572872 | tf_op jit(solution)/shard_map/ppermute | solution.py:36
  222.3 16.2 %collective-permute-start.31 = (bf16[32,8192]{1,0:T(8,128)(2,1)}, bf16[32,8192]{1,0:T(8,128)(2,1)}, u32[]{:S(2)}, u32[]{:S(2)}) collective-permute-start(bf16[32,8192]{1,0:T(8,128)(2,1)} %copy-done.45), channel_id=1, source_target_pairs={{0,2},{1,3},{2,0},{3,1},{4,6},{5,7},{6,4},{7,5},{8,10},{9,11},{10,... | collective-permute-start | bytes 1572872 | tf_op jit(solution)/shard_map/ppermute | solution.py:44
  224.6 50.3 %collective-permute-start.30 = (bf16[32,8192]{1,0:T(8,128)(2,1)}, bf16[32,8192]{1,0:T(8,128)(2,1)S(1)}, u32[]{:S(2)}, u32[]{:S(2)}) collective-permute-start(bf16[32,8192]{1,0:T(8,128)(2,1)} %copy-done.40), channel_id=1, source_target_pairs={{0,2},{1,3},{2,0},{3,1},{4,6},{5,7},{6,4},{7,5},{8,10},{9,11},{10,... | collective-permute-start | bytes 1572872 | tf_op jit(solution)/shard_map/ppermute | solution.py:44
  227.3 32.6 %collective-permute-start.34 = (bf16[32,8192]{1,0:T(8,128)(2,1)}, bf16[32,8192]{1,0:T(8,128)(2,1)S(1)}, u32[]{:S(2)}, u32[]{:S(2)}) collective-permute-start(bf16[32,8192]{1,0:T(8,128)(2,1)} %copy-done.42), channel_id=1, source_target_pairs={{0,2},{1,3},{2,0},{3,1},{4,6},{5,7},{6,4},{7,5},{8,10},{9,11},{10,... | collective-permute-start | bytes 1572872 | tf_op jit(solution)/shard_map/ppermute | solution.py:44
  235.8 60.5 %collective-permute-start.29 = (bf16[32,8192]{1,0:T(8,128)(2,1)S(1)}, bf16[32,8192]{1,0:T(8,128)(2,1)S(1)}, u32[]{:S(2)}, u32[]{:S(2)}) collective-permute-start(bf16[32,8192]{1,0:T(8,128)(2,1)S(1)} %copy-done.39), channel_id=1, source_target_pairs={{0,2},{1,3},{2,0},{3,1},{4,6},{5,7},{6,4},{7,5},{8,10},{9,11},{10,... | collective-permute-start | bytes 1572872 | tf_op jit(solution)/shard_map/ppermute | solution.py:44
  237.3 37.5 %copy-start.36 = (bf16[32,8192]{1,0:T(8,128)(2,1)S(1)}, bf16[32,8192]{1,0:T(8,128)(2,1)}, u32[]{:S(2)}) copy-start(bf16[32,8192]{1,0:T(8,128)(2,1)} %copy-done.35) | copy-start | bytes 1572868
  238.5 23.5 %collective-permute-start.22 = (bf16[32,8192]{1,0:T(8,128)(2,1)S(1)}, bf16[32,8192]{1,0:T(8,128)(2,1)S(1)}, u32[]{:S(2)}, u32[]{:S(2)}) collective-permute-start(bf16[32,8192]{1,0:T(8,128)(2,1)S(1)} %pad_maximum_fusion.2), channel_id=1, source_target_pairs={{0,4},{1,5},{2,6},{3,7},{4,8},{5,9},{6,10},{7,11},{8,12},{9,13},{1... | collective-permute-start | bytes 1572872 | tf_op jit(solution)/shard_map/ppermute | solution.py:36
  241.3 45.4 %copy-start.34 = (bf16[32,8192]{1,0:T(8,128)(2,1)S(1)}, bf16[32,8192]{1,0:T(8,128)(2,1)}, u32[]{:S(2)}) copy-start(bf16[32,8192]{1,0:T(8,128)(2,1)} %copy-done.33) | copy-start | bytes 1572868
  259.9 14.9 %collective-permute-start.24 = (bf16[32,8192]{1,0:T(8,128)(2,1)S(1)}, bf16[32,8192]{1,0:T(8,128)(2,1)S(1)}, u32[]{:S(2)}, u32[]{:S(2)}) collective-permute-start(bf16[32,8192]{1,0:T(8,128)(2,1)S(1)} %pad_maximum_fusion.3), channel_id=1, source_target_pairs={{0,12},{1,13},{2,14},{3,15},{4,0},{5,1},{6,2},{7,3},{8,4},{9,5},{1... | collective-permute-start | bytes 1572872 | tf_op jit(solution)/shard_map/ppermute | solution.py:40
  262.1 24.9 %collective-permute-start.28 = (bf16[32,8192]{1,0:T(8,128)(2,1)S(1)}, bf16[32,8192]{1,0:T(8,128)(2,1)S(1)}, u32[]{:S(2)}, u32[]{:S(2)}) collective-permute-start(bf16[32,8192]{1,0:T(8,128)(2,1)S(1)} %add_convert_fusion.5), channel_id=1, source_target_pairs={{0,12},{1,13},{2,14},{3,15},{4,0},{5,1},{6,2},{7,3},{8,4},{9,5},{1... | collective-permute-start | bytes 1572872 | tf_op jit(solution)/shard_map/ppermute | solution.py:40
  274.7 11.1 %collective-permute-start.32 = (bf16[32,8192]{1,0:T(8,128)(2,1)S(1)}, bf16[32,8192]{1,0:T(8,128)(2,1)S(1)}, u32[]{:S(2)}, u32[]{:S(2)}) collective-permute-start(bf16[32,8192]{1,0:T(8,128)(2,1)S(1)} %add_convert_fusion.3), channel_id=1, source_target_pairs={{0,4},{1,5},{2,6},{3,7},{4,8},{5,9},{6,10},{7,11},{8,12},{9,13},{1... | collective-permute-start | bytes 1572872 | tf_op jit(solution)/shard_map/ppermute | solution.py:36
  274.9 21.4 %collective-permute-start.35 = (bf16[32,8192]{1,0:T(8,128)(2,1)S(1)}, bf16[32,8192]{1,0:T(8,128)(2,1)S(1)}, u32[]{:S(2)}, u32[]{:S(2)}) collective-permute-start(bf16[32,8192]{1,0:T(8,128)(2,1)S(1)} %add_convert_fusion.1), channel_id=1, source_target_pairs={{0,12},{1,13},{2,14},{3,15},{4,0},{5,1},{6,2},{7,3},{8,4},{9,5},{1... | collective-permute-start | bytes 1572872 | tf_op jit(solution)/shard_map/ppermute | solution.py:40
  285.8 9.2 %collective-permute-start.25 = (bf16[32,8192]{1,0:T(8,128)(2,1)S(1)}, bf16[32,8192]{1,0:T(8,128)(2,1)S(1)}, u32[]{:S(2)}, u32[]{:S(2)}) collective-permute-start(bf16[32,8192]{1,0:T(8,128)(2,1)S(1)} %add_convert_fusion.6), channel_id=1, source_target_pairs={{0,2},{1,3},{2,0},{3,1},{4,6},{5,7},{6,4},{7,5},{8,10},{9,11},{10,... | collective-permute-start | bytes 1572872 | tf_op jit(solution)/shard_map/ppermute | solution.py:44
  286.8 10.5 %collective-permute-start.33 = (bf16[32,8192]{1,0:T(8,128)(2,1)S(1)}, bf16[32,8192]{1,0:T(8,128)(2,1)S(1)}, u32[]{:S(2)}, u32[]{:S(2)}) collective-permute-start(bf16[32,8192]{1,0:T(8,128)(2,1)S(1)} %add_convert_fusion.2), channel_id=1, source_target_pairs={{0,4},{1,5},{2,6},{3,7},{4,8},{5,9},{6,10},{7,11},{8,12},{9,13},{1... | collective-permute-start | bytes 1572872 | tf_op jit(solution)/shard_map/ppermute | solution.py:36
  (52 other events, 329.2 us)
